TPU v7x, 1024 devices: a whole 4x4x32 slice. The times are simulated.
1024 devices in a mesh: row: 64 (over z, core), col: 16 (over y, x).
Axes of the slice: x: 4, y: 4, z: 32, core: 2. Of those that a mesh axis runs over, the one named last changes fastest.
Arguments:
- tensor: bfloat16 [4096, 65536], P('row', 'col'), may hold values from -6 to 6
- occ_panels: bfloat16 [1024, 8192], P(('row', 'col')), may hold values from -0.75 to 0.75
- virt_panels: bfloat16 [1024, 4096], P(('row', 'col')), may hold values from -0.75 to 0.75
- b_owner: int32 [4096, 1], P('row'), may hold values from 0 to 63; in each aligned block of 64 rows (0 to 63, 64 to 127, ...) at most 2 rows name the same one
- b_local: int32 [4096, 2], P('row'), may hold values from 0 to 15
Outputs:
- contracted: bfloat16 [4096, 131072], P('row', 'col')
Inputs may be any that keep to these rules, and one draw needn't show every extreme that they name: `b_owner`: in each aligned block of 64 rows (the rows of one device) no owner appears more than 2 times, and some owner appears exactly 2 times.
All inputs are finite; a program needn't handle non-finite values.
Results may differ from a plain program's by a relative error of at most 0.0049.
Values may be sent and summed in bfloat16 or wider, within the bound.
A program may use at most 32 MiB of HBM per device.

v0:
```python
import jax
import jax.numpy as jnp
from jax import lax
from jax.sharding import PartitionSpec as P

BLK = 64
KO = 2
CAP = 2


def on_device(tensor, occ_panels, virt_panels, b_owner, b_local):
    row_count = tensor.shape[0]
    groups = lax.axis_size("row")
    panel_width = KO * BLK
    occ_row = lax.all_gather(occ_panels, "col", axis=0, tiled=True)
    occ_chosen = occ_row[b_local[:, 0]].reshape(row_count, BLK, panel_width)
    blocks = tensor.reshape(row_count, BLK, BLK)
    products = jnp.einsum(
        "tnm,tmx->tnx", blocks, occ_chosen, preferred_element_type=jnp.float32
    ).astype(jnp.bfloat16)
    virt_row = lax.all_gather(virt_panels, "col", axis=0, tiled=True)
    owners = b_owner[:, 0]
    local_nu = b_local[:, 1]
    marked = (owners[:, None] == jnp.arange(groups, dtype=jnp.int32)[None, :]).astype(jnp.int32)
    before = jnp.cumsum(marked, 0) - marked
    ranked = jnp.sum(before * marked, 1)
    placed = owners * CAP + ranked
    labels = jnp.zeros((groups * CAP,), jnp.int32).at[placed].set(local_nu).reshape(groups, CAP)
    outgoing = jnp.zeros((groups * CAP, BLK, panel_width), jnp.bfloat16).at[placed].set(products)
    outgoing = outgoing.reshape(groups, CAP, BLK, panel_width)
    arrived = lax.all_to_all(outgoing, "row", split_axis=0, concat_axis=0, tiled=True)
    wanted = lax.all_to_all(labels, "row", split_axis=0, concat_axis=0, tiled=True)
    panels = virt_row[wanted].reshape(wanted.shape + (BLK, BLK))
    result = jnp.einsum(
        "gsnx,gsny->gsxy", arrived, panels, preferred_element_type=jnp.float32
    ).astype(jnp.bfloat16)
    result = result.reshape(result.shape[0], result.shape[1], panel_width * BLK)
    returned = lax.all_to_all(result, "row", split_axis=0, concat_axis=0, tiled=True)
    finished = returned.reshape(groups * CAP, panel_width * BLK)[placed]
    return finished


def solution(mesh):
    placed = (
        P("row", "col"),
        P(("row", "col"), None),
        P(("row", "col"), None),
        P("row", None),
        P("row", None),
    )
    return jax.shard_map(
        on_device, mesh=mesh, in_specs=placed, out_specs=P("row", "col"), check_vma=False
    )
```

profile of v0, /device:TPU:2, one launch (start us, length us, event | category | flops | bytes accessed | tf_op | source)
XLA Modules:
  0.0 519.9 jit_solution(17895468107874425164)
XLA Ops:
  0.0 0.7 fusion.1
  0.7 0.1 reduce_window_sum.11
  0.8 0.8 select_reduce_fusion
  1.7 0.8 slice_bitcast_fusion
  2.4 0.8 scatter_custom_fusion.1
  3.2 0.8 all_to_all.15
  4.0 29.4 %all-to-all-start.1 = ((s32[64,1,2]{2,1,0:T(1,128)}), s32[64,1,2]{2,1,0:T(1,128)S(1)}, u32[]{:S(2)}, u32[]{:S(2)}) async-start(s32[64,1,2]{2,1,0:T(1,128)} %bitcast.9), calls=%async_computation.1 | async-start | bytes 65536 | tf_op jit(solution)/shard_map/all_to_all | solution.py:32
  33.3 24.2 %all-gather = bf16[16,1,8192]{2,1,0:T(2,128)(2,1)S(1)} all-gather(bf16[1,1,8192]{2,1,0:T(2,128)(2,1)} %bitcast.39), channel_id=1, replica_groups=mesh['row'=64,'col'=16] {'col'}, dimensions={0}, use_global_device_ids=true | all-gather | bytes 278528 | tf_op jit(solution)/shard_map/all_gather | solution.py:15
  57.5 0.3 copy.34
  57.8 1.2 gather_fusion
  59.0 0.3 copy.31
  59.3 2.1 reshape.52
  61.4 0.4 fusion
  61.8 1.9 broadcast_in_dim.4
  63.7 8.2 %scatter_fusion = bf16[128,64,128]{2,1,0:T(8,128)(2,1)} fusion(bf16[128,64,128]{2,1,0:T(8,128)(2,1)} %broadcast_in_dim.4, s32[64]{0:T(128)S(1)} %get-tuple-element.7, bf16[64,64,128]{2,1,0:T(8,128)(2,1)S(1)} %fusion), kind=kCustom, calls=%fused_computation.3 | custom fusion | bytes 3145984 | tf_op jit(solution)/shard_map/scatter | solution.py:29
  71.8 0.0 all-to-all-done.1
  71.8 0.0 copy-start
  71.8 22.5 %all-to-all-start = ((bf16[64,2,64,128]{3,2,1,0:T(8,128)(2,1)}), bf16[64,2,64,128]{3,2,1,0:T(8,128)(2,1)}, u32[]{:S(2)}, u32[]{:S(2)}) async-start(bf16[64,2,64,128]{3,2,1,0:T(8,128)(2,1)} %bitcast.6), calls=%async_computation | async-start | bytes 4194304 | tf_op jit(solution)/shard_map/all_to_all | solution.py:31
  94.4 0.0 copy-done
  94.4 22.1 %all-gather.1 = bf16[16,1,4096]{2,1,0:T(2,128)(2,1)S(1)} all-gather(bf16[1,1,4096]{2,1,0:T(2,128)(2,1)S(1)} %bitcast.40), channel_id=1, replica_groups=mesh['row'=64,'col'=16] {'col'}, dimensions={0}, use_global_device_ids=true | all-gather | bytes 139264 | tf_op jit(solution)/shard_map/all_gather | solution.py:21
  116.5 0.1 copy.35
  116.7 0.1 copy.21
  116.7 0.1 copy.22
  116.8 0.1 reshape.67
  117.0 1.2 gather_fusion.1
  118.2 3.3 reshape.54
  121.5 173.3 %all-to-all-done = bf16[64,2,64,128]{3,2,1,0:T(8,128)(2,1)} async-done(((bf16[64,2,64,128]{3,2,1,0:T(8,128)(2,1)}), bf16[64,2,64,128]{3,2,1,0:T(8,128)(2,1)}, u32[]{:S(2)}, u32[]{:S(2)}) %all-to-all-start) | async-done | bytes 2097184 | tf_op jit(solution)/shard_map/all_to_all | solution.py:31
  294.8 3.1 convolution_convert_fusion
  297.9 3.2 copy.27
  301.0 7.9 %reshape.103 = bf16[64,2,8192]{2,1,0:T(2,128)(2,1)} reshape(bf16[64,2,128,64]{3,2,1,0:T(8,128)(2,1)} %copy.27) | data formatting | bytes 4194304 | tf_op jit(solution)/shard_map/reshape | solution.py:37
  308.9 5.6 %all-to-all-start.2 = ((bf16[64,2,8192]{2,1,0:T(2,128)(2,1)}), bf16[64,2,8192]{2,1,0:T(2,128)(2,1)}, u32[]{:S(2)}, u32[]{:S(2)}) async-start(bf16[64,2,8192]{2,1,0:T(2,128)(2,1)} %reshape.103), calls=%async_computation.2 | async-start | bytes 4194304 | tf_op jit(solution)/shard_map/all_to_all | solution.py:38
  314.5 200.4 %all-to-all-done.2 = bf16[64,2,8192]{2,1,0:T(2,128)(2,1)} async-done(((bf16[64,2,8192]{2,1,0:T(2,128)(2,1)}), bf16[64,2,8192]{2,1,0:T(2,128)(2,1)}, u32[]{:S(2)}, u32[]{:S(2)}) %all-to-all-start.2) | async-done | bytes 2097184 | tf_op jit(solution)/shard_map/all_to_all | solution.py:38
  514.9 2.7 reshape.56
  517.7 2.2 gather_fusion.2
  (4 shorter events, 0.0 us)
Async XLA Ops:
  4.0 67.8 %all-to-all-start.1 = ((s32[64,1,2]{2,1,0:T(1,128)}), s32[64,1,2]{2,1,0:T(1,128)S(1)}, u32[]{:S(2)}, u32[]{:S(2)}) async-start(s32[64,1,2]{2,1,0:T(1,128)} %bitcast.9), calls=%async_computation.1 | async-start | bytes 65536 | tf_op jit(solution)/shard_map/all_to_all | solution.py:32
  71.8 22.6 %copy-start = (bf16[1,4096]{1,0:T(2,128)(2,1)S(1)}, bf16[1,4096]{1,0:T(2,128)(2,1)}, u32[]{:S(2)}) copy-start(bf16[1,4096]{1,0:T(2,128)(2,1)} %param.7) | copy-start | bytes 24580
  71.8 223.0 %all-to-all-start = ((bf16[64,2,64,128]{3,2,1,0:T(8,128)(2,1)}), bf16[64,2,64,128]{3,2,1,0:T(8,128)(2,1)}, u32[]{:S(2)}, u32[]{:S(2)}) async-start(bf16[64,2,64,128]{3,2,1,0:T(8,128)(2,1)} %bitcast.6), calls=%async_computation | async-start | bytes 4194304 | tf_op jit(solution)/shard_map/all_to_all | solution.py:31
  308.9 206.0 %all-to-all-start.2 = ((bf16[64,2,8192]{2,1,0:T(2,128)(2,1)}), bf16[64,2,8192]{2,1,0:T(2,128)(2,1)}, u32[]{:S(2)}, u32[]{:S(2)}) async-start(bf16[64,2,8192]{2,1,0:T(2,128)(2,1)} %reshape.103), calls=%async_computation.2 | async-start | bytes 4194304 | tf_op jit(solution)/shard_map/all_to_all | solution.py:38
where the time goes:
time: 521 us; the launch traced here: 520 us
  waiting for transfers between devices  374 us (72%)
  starting transfers between devices  57.4 us (11%)
  blocking collectives  46.3 us (9%)
  local copies, waits for them, and re-layouts  36.3 us (7%)
    all_to_all x1, waiting for transfers between devices, on_device(): lax.all_to_all(result, 'row', split_axis=0, concat_axis=0, tiled=True)  200 us
    all_to_all x1, waiting for transfers between devices, on_device(): lax.all_to_all(outgoing, 'row', split_axis=0, concat_axis=0, tiled=True)  173 us
    all_to_all x1, starting transfers between devices, on_device(): lax.all_to_all(labels, 'row', split_axis=0, concat_axis=0, tiled=True)  29.4 us
    all_gather x1, blocking collectives, on_device(): occ_row = lax.all_gather(occ_panels, 'col', axis=0, tiled=True)  24.2 us
    all_to_all x1, starting transfers between devices, on_device(): lax.all_to_all(outgoing, 'row', split_axis=0, concat_axis=0, tiled=True)  22.5 us
    all_gather x1, blocking collectives, on_device(): virt_row = lax.all_gather(virt_panels, 'col', axis=0, tiled=True)  22.1 us
    reshape x2, local copies, waits for them, and re-layouts, on_device(): result = result.reshape(result.shape[0], result.shape[1], panel_width * BLK)  11.1 us
  transfers between devices with their start and end apart: 3, of which 2 were waited for; matrix products, arithmetic and copies ran while one was open for 4% of the time, Pallas kernels for 0%

commit v1 on v0

v1 whole, which is shorter than its diff:
```python
import jax
import jax.numpy as jnp
from jax import lax
from jax.experimental import pallas as pl
from jax.experimental.pallas import tpu as pltpu
from jax.sharding import PartitionSpec as P

MESH = pl.DeviceIdType.MESH
BF = jnp.bfloat16
F32 = jnp.float32
I32 = jnp.int32

T = 64
GROUPS = 64
PLANES = 32
COLS = 16
FAR = 11
NEAR = 5
SERVED = 2 * NEAR + 1
SLOTS = 16
ENTRIES = SERVED * SLOTS
PADDED = 256
HALF = 32

NT = (((1,), (1,)), ((), ()))


def iota(shape, axis):
    return lax.broadcasted_iota(I32, shape, axis)


def one_hot(cond):
    return jnp.where(cond, 1.0, 0.0)


def dot(a, b):
    return jnp.dot(a, b, preferred_element_type=F32)


def swap_halves(v):
    return jnp.concatenate([v[:, 64:], v[:, :64]], axis=1)


def kernel(tensor, occ, virt, owner, local, local_s, out,
           tensor_v, tensor_f, occ_all, occ_t, middle, panels, far, asked, asks, replies, near, chosen,
           chosen_a, chosen_b, out_f, out_v,
           tensor_sem, out_sem,
           panel_send, panel_recv, occ_send, occ_recv, far_send, far_recv, ask_send, ask_recv,
           near_send, near_recv, last_send, last_recv):
    r, c = lax.axis_index("row"), lax.axis_index("col")
    z, core = lax.div(r, 2), lax.rem(r, 2)

    def at_plane(offset, on_core):
        return 2 * lax.rem(z + offset + PLANES, PLANES) + on_core

    def in_plane(i):
        return (r, lax.rem(c + i, COLS))

    tensor_copy = pltpu.make_async_copy(tensor, tensor_v, tensor_sem)
    tensor_copy.start()

    barrier = pltpu.get_barrier_semaphore()
    partners = [in_plane(i) for i in range(1, COLS)]
    partners += [(at_plane(o, core), c) for o in range(-NEAR, NEAR + 1) if o != 0]
    far_partners = [(at_plane(0, 1 - core), c)]
    far_partners += [(at_plane(o, lax.rem(core + k, 2)), c) for o in (-FAR, FAR) for k in (0, 1)]
    partners += far_partners
    for partner in far_partners + partners[:-len(far_partners)]:
        pl.semaphore_signal(barrier, inc=1, device_id=partner, device_id_type=MESH)

    owner_col = owner[...]
    same = iota((T, 128), 0) == iota((T, 128), 1)
    owner_row = jnp.sum(jnp.where(same, owner_col, 0), axis=0, keepdims=True)
    earlier = iota((T, 128), 1) < iota((T, 128), 0)
    rank_col = jnp.sum(jnp.where((owner_col == owner_row) & earlier, 1, 0), axis=1, keepdims=True)
    e = iota((T, PADDED), 1)
    server, w = e >> 4, e & 15
    source = w >> 2
    plane = (z + server - NEAR + FAR * (source - 1) + 2 * PLANES) & (PLANES - 1)
    group = 2 * plane + ((w >> 1) & 1)
    used = (e < ENTRIES) & (w < 12) & ((server != 0) | (source != 0))
    picks = one_hot(used & (owner_col == group) & (rank_col == (w & 1)))
    position = one_hot((iota((T, 128), 1) & 15) == local[:, 1:2]).astype(BF)
    wanted = dot(picks.T.astype(BF), position)
    row, lane = iota((PADDED, 128), 0), iota((PADDED, 128), 1)
    wanted = jnp.where(((row & 15) >> 1) == (lane >> 4), wanted, 0.0)
    asks[...] = wanted[:ENTRIES].astype(BF)
    far[96:128, :] = jnp.zeros((32, 256), BF)
    near[ENTRIES:, :] = jnp.zeros((PADDED - ENTRIES, 256), BF)

    panels[pl.ds(pl.multiple_of(c * 32, 32), 32), :] = virt[...]
    occ_all[c] = occ[...]

    pl.semaphore_wait(barrier, len(partners))

    panel_copies = []
    for i in range(1, COLS):
        rows = pl.ds(pl.multiple_of(c * 32, 32), 32)
        panel_copies.append(pltpu.make_async_remote_copy(
            virt, panels.at[rows, :], panel_send.at[i], panel_recv.at[i],
            device_id=in_plane(i), device_id_type=MESH))
        panel_copies[-1].start()
    ask_copies = []
    for k in range(SERVED):
        if k == NEAR:
            continue
        rows = pl.ds(k * SLOTS, SLOTS)
        ask_copies.append(pltpu.make_async_remote_copy(
            asks.at[rows, :], asked.at[rows, :], ask_send.at[k], ask_recv.at[k],
            device_id=(at_plane(k - NEAR, core), c), device_id_type=MESH))
        ask_copies[-1].start()
    asked[NEAR * SLOTS:(NEAR + 1) * SLOTS, :] = asks[NEAR * SLOTS:(NEAR + 1) * SLOTS, :]
    occ_copies = []
    for i in range(1, COLS):
        occ_copies.append(pltpu.make_async_remote_copy(
            occ, occ_all.at[c], occ_send.at[i], occ_recv.at[i],
            device_id=in_plane(i), device_id_type=MESH))
        occ_copies[-1].start()

    tensor_copy.wait()
    for i in range(32):
        tensor_f[i * T:(i + 1) * T, :] = tensor_v[:, i * 128:(i + 1) * 128].astype(F32)

    for copy in panel_copies:
        copy.wait()
    line, entry = iota((COLS, 512), 0), iota((COLS, 512), 1)
    held = panels[...]
    piece = [dot(one_hot((entry >> 5 == line) & ((entry & 31) == h * 16 + c)).astype(BF), held) for h in (0, 1)]
    own = pl.ds(pl.multiple_of((2 + core) * COLS, COLS), COLS)
    far[own, :] = jnp.concatenate(piece, axis=1).astype(BF)

    far_copies = []
    for n, (partner, source_there) in enumerate(zip(far_partners, (1, 2, 2, 0, 0))):
        rows = pl.ds(pl.multiple_of((2 * source_there + core) * COLS, COLS), COLS)
        far_copies.append(pltpu.make_async_remote_copy(
            far.at[own, :], far.at[rows, :], far_send.at[n], far_recv.at[n],
            device_id=partner, device_id_type=MESH))
        far_copies[-1].start()

    for copy in occ_copies:
        copy.wait()
    x_out, x_in = iota((128, 128), 0), iota((128, 128), 1)
    order = one_hot(x_in == 2 * (x_out & 63) + (x_out >> 6)).astype(BF)

    @pl.loop(0, COLS)
    def _(i):
        turned = lax.dot_general(order, occ_all[i], NT, preferred_element_type=F32)
        occ_t[i] = turned.astype(BF)

    def first(t):
        block = tensor_f[pl.ds(t, 32, stride=T), :]
        block = jnp.concatenate([block[:, :64], block[:, 64:]], axis=0).astype(BF)
        product = lax.dot_general(occ_t[local_s[t, 0]], block, NT, preferred_element_type=F32)
        middle[t] = jnp.concatenate([product[:64], product[64:]], axis=1).astype(BF)

    pl.loop(0, HALF, unroll=4)(first)

    for copy in far_copies:
        copy.wait()
    for copy in ask_copies:
        copy.wait()
    replies[...] = dot(asked[...], far[...]).astype(BF)
    near_copies = []
    for k in (0, 10, 1, 9, 2, 8, 3, 7, 4, 6):
        rows = pl.ds(k * SLOTS, SLOTS)
        near_copies.append(pltpu.make_async_remote_copy(
            replies.at[rows, :], near.at[rows, :], near_send.at[k], near_recv.at[k],
            device_id=(at_plane(NEAR - k, core), c), device_id_type=MESH))
        near_copies[-1].start()
    near[NEAR * SLOTS:(NEAR + 1) * SLOTS, :] = replies[NEAR * SLOTS:(NEAR + 1) * SLOTS, :]

    pl.loop(HALF, T, unroll=4)(first)

    for copy in near_copies:
        copy.wait()
    chosen[c] = dot(picks.astype(BF), near[...]).astype(BF)
    last_copies = []
    for h in (0, 1):
        for i in range(1, COLS):
            rows = pl.ds(h * HALF, HALF)
            last_copies.append(pltpu.make_async_remote_copy(
                chosen.at[c, rows, :], chosen.at[c, rows, :], last_send.at[h, i], last_recv.at[h, i],
                device_id=in_plane(i), device_id_type=MESH))
            last_copies[-1].start()

    low = iota((32, 128), 1) < 64
    out_copies = []
    for h in (0, 1):
        for copy in last_copies[h * 15:(h + 1) * 15]:
            copy.wait()

        @pl.loop(0, COLS)
        def _(i):
            part = chosen[i, h * HALF:(h + 1) * HALF, :].astype(F32)
            rows = pl.ds(pl.multiple_of(i * T + h * HALF, HALF), HALF)
            chosen_a[rows, :] = part[:, :128]
            chosen_b[rows, :] = part[:, 128:]

        @pl.loop(h * HALF, (h + 1) * HALF, unroll=4)
        def _(t):
            panel = jnp.concatenate(
                [chosen_a[pl.ds(t, COLS, stride=T), :], chosen_b[pl.ds(t, COLS, stride=T), :]], axis=0)
            turned = swap_halves(panel)
            both = jnp.concatenate(
                [jnp.where(low, panel, 0.0), jnp.where(low, turned, 0.0),
                 jnp.where(low, 0.0, turned), jnp.where(low, 0.0, panel)], axis=0).astype(BF)
            out_f[pl.ds(t, T, stride=T), :] = dot(middle[t], both)

        for x in range(64):
            out_v[h * HALF:(h + 1) * HALF, x * 128:(x + 1) * 128] = (
                out_f[x * T + h * HALF:x * T + (h + 1) * HALF, :].astype(BF))
        rows = pl.ds(h * HALF, HALF)
        out_copies.append(pltpu.make_async_copy(out_v.at[rows, :], out.at[rows, :], out_sem.at[h]))
        out_copies[-1].start()
    for copy in out_copies:
        copy.wait()


def on_device(tensor, occ_panels, virt_panels, b_owner, b_local):
    hbm = pl.BlockSpec(memory_space=pl.ANY)
    vmem = pl.BlockSpec(memory_space=pltpu.VMEM)
    smem = pl.BlockSpec(memory_space=pltpu.SMEM)
    dma = pltpu.SemaphoreType.DMA
    return pl.pallas_call(
        kernel,
        out_shape=jax.ShapeDtypeStruct((T, 8192), BF),
        in_specs=[hbm, vmem, vmem, vmem, vmem, smem],
        out_specs=hbm,
        scratch_shapes=[
            pltpu.VMEM((T, 4096), BF),
            pltpu.VMEM((32 * T, 128), F32),
            pltpu.VMEM((COLS, 64, 128), BF),
            pltpu.VMEM((COLS, 128, 64), BF),
            pltpu.VMEM((T, 64, 128), BF),
            pltpu.VMEM((COLS * 32, 128), BF),
            pltpu.VMEM((128, 256), BF),
            pltpu.VMEM((ENTRIES, 128), BF),
            pltpu.VMEM((ENTRIES, 128), BF),
            pltpu.VMEM((ENTRIES, 256), BF),
            pltpu.VMEM((PADDED, 256), BF),
            pltpu.VMEM((COLS, T, 256), BF),
            pltpu.VMEM((COLS * T, 128), F32),
            pltpu.VMEM((COLS * T, 128), F32),
            pltpu.VMEM((64 * T, 128), F32),
            pltpu.VMEM((T, 8192), BF),
            dma, dma((2,)),
            dma((COLS,)), dma((COLS,)), dma((COLS,)), dma((COLS,)),
            dma((6,)), dma((6,)), dma((SERVED,)), dma((SERVED,)),
            dma((SERVED,)), dma((SERVED,)), dma((2, COLS)), dma((2, COLS)),
        ],
        compiler_params=pltpu.CompilerParams(
            collective_id=0, has_side_effects=True, vmem_limit_bytes=32 << 20),
        cost_estimate=pl.CostEstimate(flops=300_000_000, bytes_accessed=3_000_000, transcendentals=0),
    )(tensor, occ_panels.reshape(64, 128), virt_panels.reshape(32, 128), b_owner, b_local, b_local)


def solution(mesh):
    placed = (
        P("row", "col"),
        P(("row", "col"), None),
        P(("row", "col"), None),
        P("row", None),
        P("row", None),
    )
    return jax.shard_map(
        on_device, mesh=mesh, in_specs=placed, out_specs=P("row", "col"), check_vma=False
    )
```

time: 521 us -> 67.6 us (0.13)
  the two profiles are of different devices: /device:TPU:2 before, /device:TPU:4 now
where the time goes in v1:
time: 67.6 us; the launch traced here: 67.3 us
  Pallas kernels  62.2 us (92%)
  local copies, waits for them, and re-layouts  3.44 us (5%)
  other arithmetic  1.62 us (2%)
    pallas_call x1, Pallas kernels, on_device(): pl.pallas_call(kernel, out_shape=jax.ShapeDtypeStruct((T, 8192), BF), in_...  62.2 us
    unnamed x9, local copies, waits for them, and re-layouts  3.44 us
    unnamed x2, other arithmetic  1.62 us

profile of v1, /device:TPU:4, one launch (start us, length us, event | category | flops | bytes accessed | tf_op | source)
XLA Modules:
  0.0 67.3 jit_solution(11033551272353756266)
XLA Ops:
  0.0 0.8 %reduce.1 = bf16[4096]{0:T(1024)(128)(2,1)S(1)} reduce(bf16[1,4096]{1,0:T(2,128)(2,1)} %param.7, bf16[]{:T(256)} %constant.2), dimensions={0}, to_apply=%param.7.reduce_sub_computation | reduce | bytes 16386 | tf_op args[2]
  0.8 0.8 %reduce = bf16[8192]{0:T(1024)(128)(2,1)S(1)} reduce(bf16[1,8192]{1,0:T(2,128)(2,1)} %param.6, bf16[]{:T(256)} %constant.2), dimensions={0}, to_apply=%param.6.reduce_sub_computation | reduce | bytes 32770 | tf_op args[1]
  1.6 0.0 copy-start.2
  1.6 0.6 copy-done.2
  2.3 0.0 copy-start.1
  2.3 0.1 copy.6.owner
  2.4 0.6 copy-done.1
  3.0 0.1 copy.7.local.local_s
  3.1 0.0 copy-start
  3.1 1.0 %copy-done = bf16[64,4096]{1,0:T(8,128)(2,1)S(1)} copy-done((bf16[64,4096]{1,0:T(8,128)(2,1)S(1)}, bf16[64,4096]{1,0:T(8,128)(2,1)}, u32[]{:S(2)}) %copy-start) | copy-done | bytes 524312
  4.1 62.2 %shard_map.55 = bf16[64,8192]{1,0:T(8,128)(2,1)S(1)} custom-call(bf16[64,4096]{1,0:T(8,128)(2,1)S(1)} %copy-done, bf16[64,128]{1,0:T(8,128)(2,1)S(1)} %bitcast.2, bf16[32,128]{1,0:T(8,128)(2,1)S(1)} %bitcast.3, s32[64,1]{1,0:T(8,128)S(1)} %copy.6.owner, s32[64,2]{1,0:T(8,128)S(1)} %copy.7.local.local_s, s32[64,2]{1,0:T(8,128)S(1)} %copy.7.local.local_s), custom_call_target="tpu_custom_call" | custom-call | flops 300000000 | bytes 3000000 | tf_op jit(solution)/shard_map/pallas_call | solution.py:224
  66.3 1.0 %copy.10 = bf16[64,8192]{1,0:T(8,128)(2,1)} copy(bf16[64,8192]{1,0:T(8,128)(2,1)S(1)} %shard_map.55) | data formatting | bytes 2097152
Async XLA Ops:
  1.6 0.7 copy-start.2
  2.3 0.7 %copy-start.1 = (s32[64,2]{0,1:T(2,128)S(1)}, s32[64,2]{0,1:T(2,128)}, u32[]{:S(2)}) copy-start(s32[64,2]{0,1:T(2,128)} %param.9) | copy-start | bytes 1540
  3.1 1.0 %copy-start = (bf16[64,4096]{1,0:T(8,128)(2,1)S(1)}, bf16[64,4096]{1,0:T(8,128)(2,1)}, u32[]{:S(2)}) copy-start(bf16[64,4096]{1,0:T(8,128)(2,1)} %tensor.1) | copy-start | bytes 1572868

commit v2 on v0

v2 whole, which is shorter than its diff:
```python
import jax
import jax.numpy as jnp
from jax import lax
from jax.experimental import pallas as pl
from jax.experimental.pallas import tpu as pltpu
from jax.sharding import PartitionSpec as P

MESH = pl.DeviceIdType.MESH
BF = jnp.bfloat16
F32 = jnp.float32
I32 = jnp.int32

T = 64
GROUPS = 64
PLANES = 32
COLS = 16
FAR = 10
NEAR = 6
SERVED = 2 * NEAR + 1
SLOTS = 16
ENTRIES = SERVED * SLOTS
PADDED = 256
HALF = 32
PARTS = 2
PART = T // PARTS
STEP = 72

NT = (((1,), (1,)), ((), ()))


def iota(shape, axis):
    return lax.broadcasted_iota(I32, shape, axis)


def one_hot(cond):
    return jnp.where(cond, 1.0, 0.0)


def dot(a, b):
    return jnp.dot(a, b, preferred_element_type=F32)


def swap_halves(v):
    return jnp.concatenate([v[:, 64:], v[:, :64]], axis=1)


def kernel(tensor, occ, virt, owner, local, out,
           owner_v, local_v, local_s, occ_v, virt_v, lines,
           tensor_v, tensor_f, occ_all, occ_t, middle, panels, far, asked, asks, replies, near, chosen,
           chosen_f, out_f,
           in_sem, relay,
           panel_send, panel_recv, occ_send, occ_recv, far_send, far_recv, ask_send, ask_recv,
           near_send, near_recv, even_send, even_recv, odd_send, odd_recv):
    r, c = lax.axis_index("row"), lax.axis_index("col")
    z, core = lax.div(r, 2), lax.rem(r, 2)

    def at_plane(offset, on_core):
        return 2 * lax.rem(z + offset + PLANES, PLANES) + on_core

    def in_plane(i):
        return (r, lax.rem(c + i, COLS))

    def send(source, target, send_sem, recv_sem, partner):
        copy = pltpu.make_async_remote_copy(source, target, send_sem, recv_sem,
                                            device_id=partner, device_id_type=MESH)
        copy.start()
        return copy

    in_copies = [
        pltpu.make_async_copy(source, target, in_sem.at[n]) for n, (source, target) in enumerate(
            ((virt, virt_v), (occ, occ_v), (owner, owner_v), (local, local_v), (local, local_s), (tensor, tensor_v)))]
    for copy in in_copies:
        copy.start()
    virt_copy, occ_copy, owner_copy, local_copy, scalar_copy, tensor_copy = in_copies

    barrier = pltpu.get_barrier_semaphore()
    other = (at_plane(0, 1 - core), c)
    relays = [(at_plane(o, lax.rem(core + k, 2)), c) for o in (-NEAR, NEAR) for k in (0, 1)]
    partners = relays + [(at_plane(o, core), c) for o in range(1 - NEAR, NEAR) if o != 0]
    partners += [in_plane(i) for i in range(1, COLS)] + [other]
    far_partners = [(at_plane(o, lax.rem(core + k, 2)), c) for o in (-FAR, FAR) for k in (0, 1)] + [other]
    for partner in partners:
        pl.semaphore_signal(barrier, inc=1, device_id=partner, device_id_type=MESH)

    my_panel = pl.ds(pl.multiple_of(c * 32, 32), 32)
    virt_copy.wait()
    for i in range(32):
        lines[i:i + 1, :] = virt_v[:, i * 128:(i + 1) * 128].astype(F32)
    panels[my_panel, :] = lines[:32, :].astype(BF)
    line, entry = iota((COLS, 512), 0), iota((COLS, 512), 1)
    takes = [one_hot((entry >> 5 == line) & ((entry & 31) == h * 16 + c)).astype(BF) for h in (0, 1)]

    pl.semaphore_wait(barrier, len(partners))

    panel_copies = [send(panels.at[my_panel, :], panels.at[my_panel, :], panel_send.at[i], panel_recv.at[i],
                         in_plane(i)) for i in range(1, COLS)]
    for n, partner in enumerate(relays):
        pl.semaphore_signal(relay.at[n], inc=1, device_id=partner, device_id_type=MESH)
    occ_copy.wait()
    for i in range(64):
        lines[i:i + 1, :] = occ_v[:, i * 128:(i + 1) * 128].astype(F32)
    occ_all[c] = lines[...].astype(BF)

    owner_copy.wait()
    local_copy.wait()
    same = iota((T, T), 0) == iota((T, T), 1)
    owner_row = owner_v[...]
    owner_col = jnp.sum(jnp.where(same, owner_row, 0), axis=1, keepdims=True)
    local_col = jnp.sum(jnp.where(same, local_v[1:2, :], 0), axis=1, keepdims=True)
    earlier = iota((T, T), 1) < iota((T, T), 0)
    rank_col = jnp.sum(jnp.where((owner_col == owner_row) & earlier, 1, 0), axis=1, keepdims=True)
    e = iota((T, PADDED), 1)
    server, w = e >> 4, e & 15
    source = w >> 2
    away = server - NEAR + FAR * (source - 1)
    plane = (z + away + 2 * PLANES) & (PLANES - 1)
    group = 2 * plane + ((w >> 1) & 1)
    used = (e < ENTRIES) & (w < 12) & ((source == 1) | (away > NEAR) | ((away < -NEAR) & (away > -PLANES // 2)))
    picks = one_hot(used & (owner_col == group) & (rank_col == (w & 1)))
    position = one_hot((iota((T, 128), 1) & 15) == local_col).astype(BF)
    wanted = dot(picks.T.astype(BF), position)
    row, lane = iota((PADDED, 128), 0), iota((PADDED, 128), 1)
    wanted = jnp.where(((row & 15) >> 1) == (lane >> 4), wanted, 0.0)
    asks[...] = wanted[:ENTRIES].astype(BF)
    picks = picks.astype(BF)
    served = [k for k in range(SERVED) if k != NEAR]
    served.sort(key=lambda k: -abs(k - NEAR))
    mine = slice(NEAR * SLOTS, (NEAR + 1) * SLOTS)
    ask_copies = []
    for k in served:
        rows = pl.ds(k * SLOTS, SLOTS)
        ask_copies.append(send(asks.at[rows, :], asked.at[rows, :], ask_send.at[k], ask_recv.at[k],
                               (at_plane(k - NEAR, core), c)))
    asked[mine, :] = asks[mine, :]
    for h in (0, 1):
        far[h, 96:128, :] = jnp.zeros((32, 128), BF)
        near[h, ENTRIES:, :] = jnp.zeros((PADDED - ENTRIES, 128), BF)

    tensor_copy.wait()
    for i in range(32):
        tensor_f[i * STEP:i * STEP + T, :] = tensor_v[:, i * 128:(i + 1) * 128].astype(F32)

    for copy in panel_copies:
        copy.wait()
    for n in range(len(relays)):
        pl.semaphore_wait(relay.at[n], 1)

    own = pl.ds(pl.multiple_of((2 + core) * COLS, COLS), COLS)
    far_copies = []
    for h in (0, 1):
        far[h, own, :] = dot(takes[h], panels[...]).astype(BF)
        for n, (partner, source_there) in enumerate(zip(far_partners, (2, 2, 0, 0, 1))):
            rows = pl.ds(pl.multiple_of((2 * source_there + core) * COLS, COLS), COLS)
            far_copies.append(send(far.at[h, own, :], far.at[h, rows, :], far_send.at[h, n], far_recv.at[h, n],
                                   partner))

    occ_copies = [send(occ_all.at[c], occ_all.at[c], occ_send.at[i], occ_recv.at[i], in_plane(i))
                  for i in range(1, COLS)]

    for copy in ask_copies:
        copy.wait()
    near_copies = []
    for h in (0, 1):
        for copy in far_copies[h * 5:(h + 1) * 5]:
            copy.wait()
        replies[h] = dot(asked[...], far[h]).astype(BF)
        for k in served:
            rows = pl.ds(k * SLOTS, SLOTS)
            near_copies.append(send(replies.at[h, rows, :], near.at[h, rows, :], near_send.at[h, k],
                                    near_recv.at[h, k], (at_plane(NEAR - k, core), c)))
        near[h, mine, :] = replies[h, mine, :]

    for copy in occ_copies:
        copy.wait()
    scalar_copy.wait()
    x_out, x_in = iota((128, 128), 0), iota((128, 128), 1)
    order = one_hot(x_in == 2 * (x_out & 63) + (x_out >> 6)).astype(BF)

    @pl.loop(0, COLS, unroll=4)
    def _(i):
        turned = lax.dot_general(order, occ_all[i], NT, preferred_element_type=F32)
        occ_t[i] = turned.astype(BF)

    def first(t):
        block = tensor_f[pl.ds(t, 32, stride=STEP), :]
        block = jnp.concatenate([block[:, :64], block[:, 64:]], axis=0).astype(BF)
        product = lax.dot_general(occ_t[local_s[0, t]], block, NT, preferred_element_type=F32)
        middle[t] = jnp.concatenate([product[:64], product[64:]], axis=1).astype(BF)

    pl.loop(0, T, unroll=8)(first)

    n_near = len(served)
    for copy in near_copies[:n_near]:
        copy.wait()
    chosen[0, c] = dot(picks, near[0]).astype(BF)
    even_copies = [send(chosen.at[0, c], chosen.at[0, c], even_send.at[i], even_recv.at[i], in_plane(i))
                   for i in range(1, COLS)]
    for copy in near_copies[n_near:]:
        copy.wait()
    chosen[1, c] = dot(picks, near[1]).astype(BF)
    odd_copies = []
    for p in range(PARTS):
        rows = pl.ds(p * PART, PART)
        odd_copies += [send(chosen.at[1, c, rows, :], chosen.at[1, c, rows, :], odd_send.at[p, i], odd_recv.at[p, i],
                            in_plane(i)) for i in range(1, COLS)]

    low = iota((32, 128), 1) < 64

    def second(t):
        panel = jnp.concatenate([chosen_f[h, pl.ds(t, COLS, stride=STEP), :] for h in (0, 1)], axis=0)
        turned = swap_halves(panel)
        both = jnp.concatenate(
            [jnp.where(low, panel, 0.0), jnp.where(low, turned, 0.0),
             jnp.where(low, 0.0, turned), jnp.where(low, 0.0, panel)], axis=0).astype(BF)
        out_f[pl.ds(t, T, stride=STEP), :] = dot(middle[t], both)

    for copy in even_copies:
        copy.wait()
    for i in range(COLS):
        chosen_f[0, i * STEP:i * STEP + T, :] = chosen[0, i].astype(F32)
    for p in range(PARTS):
        for copy in odd_copies[p * 15:(p + 1) * 15]:
            copy.wait()
        for i in range(COLS):
            chosen_f[1, i * STEP + p * PART:i * STEP + (p + 1) * PART, :] = (
                chosen[1, i, p * PART:(p + 1) * PART, :].astype(F32))
        pl.loop(p * PART, (p + 1) * PART, unroll=16)(second)
        for x in range(64):
            out[p * PART:(p + 1) * PART, x * 128:(x + 1) * 128] = (
                out_f[x * STEP + p * PART:x * STEP + (p + 1) * PART, :].astype(BF))


def on_device(tensor, occ_panels, virt_panels, b_owner, b_local):
    hbm = pl.BlockSpec(memory_space=pltpu.HBM)
    operands = (tensor, occ_panels, virt_panels, b_owner.T, b_local.T)
    operands = [pltpu.with_memory_space_constraint(operand, pltpu.HBM) for operand in operands]
    dma = pltpu.SemaphoreType.DMA
    return pl.pallas_call(
        kernel,
        out_shape=pltpu.VMEM((T, 8192), BF),
        in_specs=[hbm] * 5,
        out_specs=pl.BlockSpec(memory_space=pltpu.VMEM),
        scratch_shapes=[
            pltpu.VMEM((1, T), I32),
            pltpu.VMEM((2, T), I32),
            pltpu.SMEM((2, T), I32),
            pltpu.VMEM((1, 8192), BF),
            pltpu.VMEM((1, 4096), BF),
            pltpu.VMEM((64, 128), F32),
            pltpu.VMEM((T, 4096), BF),
            pltpu.VMEM((32 * STEP, 128), F32),
            pltpu.VMEM((COLS, 64, 128), BF),
            pltpu.VMEM((COLS, 128, 64), BF),
            pltpu.VMEM((T, 64, 128), BF),
            pltpu.VMEM((COLS * 32, 128), BF),
            pltpu.VMEM((2, 128, 128), BF),
            pltpu.VMEM((ENTRIES, 128), BF),
            pltpu.VMEM((ENTRIES, 128), BF),
            pltpu.VMEM((2, ENTRIES, 128), BF),
            pltpu.VMEM((2, PADDED, 128), BF),
            pltpu.VMEM((2, COLS, T, 128), BF),
            pltpu.VMEM((2, COLS * STEP, 128), F32),
            pltpu.VMEM((64 * STEP, 128), F32),
            dma((6,)), pltpu.SemaphoreType.REGULAR((4,)),
            dma((COLS,)), dma((COLS,)), dma((COLS,)), dma((COLS,)),
            dma((2, 5)), dma((2, 5)), dma((SERVED,)), dma((SERVED,)),
            dma((2, SERVED)), dma((2, SERVED)),
            dma((COLS,)), dma((COLS,)), dma((PARTS, COLS)), dma((PARTS, COLS)),
        ],
        compiler_params=pltpu.CompilerParams(
            collective_id=0, has_side_effects=True, vmem_limit_bytes=32 << 20),
        cost_estimate=pl.CostEstimate(flops=300_000_000, bytes_accessed=3_000_000, transcendentals=0),
    )(*operands)


def solution(mesh):
    placed = (
        P("row", "col"),
        P(("row", "col"), None),
        P(("row", "col"), None),
        P("row", None),
        P("row", None),
    )
    return jax.shard_map(
        on_device, mesh=mesh, in_specs=placed, out_specs=P("row", "col"), check_vma=False
    )
```

time: 521 us -> 57 us (0.11)
  the two profiles are of different devices: /device:TPU:2 before, /device:TPU:8 now
where the time goes in v2:
time: 57 us; the launch traced here: 56.8 us
  Pallas kernels  55.9 us (98%)
  local copies, waits for them, and re-layouts  0.97 us (2%)
    pallas_call x1, Pallas kernels, on_device(): pl.pallas_call(kernel, out_shape=pltpu.VMEM((T, 8192), BF), in_specs=[hbm...  55.9 us

profile of v2, /device:TPU:8, one launch (start us, length us, event | category | flops | bytes accessed | tf_op | source)
XLA Modules:
  0.0 56.8 jit_solution(2463486175238664219)
XLA Ops:
  0.0 55.9 %shard_map.55 = bf16[64,8192]{1,0:T(8,128)(2,1)S(1)} custom-call(bf16[64,4096]{1,0:T(8,128)(2,1)} %tensor.1, bf16[1,8192]{1,0:T(2,128)(2,1)} %occ.1, bf16[1,4096]{1,0:T(2,128)(2,1)} %virt.1, s32[1,64]{1,0:T(1,128)} %bitcast.3, s32[2,64]{1,0:T(2,128)} %bitcast.2), custom_call_target="tpu_custom_call" | custom-call | flops 300000000 | bytes 3000000 | tf_op jit(solution)/shard_map/pallas_call | solution.py:238
  55.9 1.0 %copy.7 = bf16[64,8192]{1,0:T(8,128)(2,1)} copy(bf16[64,8192]{1,0:T(8,128)(2,1)S(1)} %shard_map.55) | data formatting | bytes 2097152

commit v3 on v2

--- a/solution.py
+++ b/solution.py
@@ -11,11 +11,12 @@
 I32 = jnp.int32
 
 T = 64
-GROUPS = 64
 PLANES = 32
+SIDE = 4
 COLS = 16
 FAR = 10
 NEAR = 6
+STAGE = FAR - NEAR
 SERVED = 2 * NEAR + 1
 SLOTS = 16
 ENTRIES = SERVED * SLOTS
@@ -25,6 +26,13 @@
 PART = T // PARTS
 STEP = 72
 
+
+def hops(i):
+    return min(i // SIDE, SIDE - i // SIDE) + min(i % SIDE, SIDE - i % SIDE)
+
+
+NEIGHBOURS = sorted(range(1, COLS), key=lambda i: -hops(i))
+
 NT = (((1,), (1,)), ((), ()))
 
 
@@ -46,7 +54,7 @@
 
 def kernel(tensor, occ, virt, owner, local, out,
            owner_v, local_v, local_s, occ_v, virt_v, lines,
-           tensor_v, tensor_f, occ_all, occ_t, middle, panels, far, asked, asks, replies, near, chosen,
+           tensor_v, tensor_f, occ_all, occ_t, middle, cuts, pieces, far, asked, asks, replies, near, chosen,
            chosen_f, out_f,
            in_sem, relay,
            panel_send, panel_recv, occ_send, occ_recv, far_send, far_recv, ask_send, ask_recv,
@@ -57,8 +65,11 @@
     def at_plane(offset, on_core):
         return 2 * lax.rem(z + offset + PLANES, PLANES) + on_core
 
+    line, place = lax.div(c, SIDE), lax.rem(c, SIDE)
+
     def in_plane(i):
-        return (r, lax.rem(c + i, COLS))
+        dy, dx = i // SIDE, i % SIDE
+        return (r, SIDE * lax.rem(line + dy, SIDE) + lax.rem(place + dx, SIDE))
 
     def send(source, target, send_sem, recv_sem, partner):
         copy = pltpu.make_async_remote_copy(source, target, send_sem, recv_sem,
@@ -69,33 +80,34 @@
     in_copies = [
         pltpu.make_async_copy(source, target, in_sem.at[n]) for n, (source, target) in enumerate(
             ((virt, virt_v), (occ, occ_v), (owner, owner_v), (local, local_v), (local, local_s), (tensor, tensor_v)))]
-    for copy in in_copies:
-        copy.start()
     virt_copy, occ_copy, owner_copy, local_copy, scalar_copy, tensor_copy = in_copies
+    virt_copy.start()
 
     barrier = pltpu.get_barrier_semaphore()
     other = (at_plane(0, 1 - core), c)
-    relays = [(at_plane(o, lax.rem(core + k, 2)), c) for o in (-NEAR, NEAR) for k in (0, 1)]
-    partners = relays + [(at_plane(o, core), c) for o in range(1 - NEAR, NEAR) if o != 0]
-    partners += [in_plane(i) for i in range(1, COLS)] + [other]
+    relays = [(at_plane(o, lax.rem(core + k, 2)), c) for o in (-STAGE, STAGE) for k in (0, 1)]
     far_partners = [(at_plane(o, lax.rem(core + k, 2)), c) for o in (-FAR, FAR) for k in (0, 1)] + [other]
-    for partner in partners:
+    partners = [(STAGE, partner) for partner in relays] + [(0, other)]
+    partners += [(abs(o), (at_plane(o, core), c)) for o in range(-NEAR, NEAR + 1) if o not in (0, STAGE, -STAGE)]
+    partners += [(hops(i), in_plane(i)) for i in NEIGHBOURS]
+    for _, partner in sorted(partners, key=lambda pair: -pair[0]):
         pl.semaphore_signal(barrier, inc=1, device_id=partner, device_id_type=MESH)
-
-    my_panel = pl.ds(pl.multiple_of(c * 32, 32), 32)
+    for copy in in_copies[1:]:
+        copy.start()
+
     virt_copy.wait()
     for i in range(32):
-        lines[i:i + 1, :] = virt_v[:, i * 128:(i + 1) * 128].astype(F32)
-    panels[my_panel, :] = lines[:32, :].astype(BF)
-    line, entry = iota((COLS, 512), 0), iota((COLS, 512), 1)
-    takes = [one_hot((entry >> 5 == line) & ((entry & 31) == h * 16 + c)).astype(BF) for h in (0, 1)]
+        cuts[i % COLS, i // COLS:i // COLS + 1, :] = virt_v[:, i * 128:(i + 1) * 128].astype(F32)
+    pieces[c] = cuts[c]
 
     pl.semaphore_wait(barrier, len(partners))
 
-    panel_copies = [send(panels.at[my_panel, :], panels.at[my_panel, :], panel_send.at[i], panel_recv.at[i],
-                         in_plane(i)) for i in range(1, COLS)]
     for n, partner in enumerate(relays):
         pl.semaphore_signal(relay.at[n], inc=1, device_id=partner, device_id_type=MESH)
+    panel_copies = []
+    for i in NEIGHBOURS:
+        partner = in_plane(i)
+        panel_copies.append(send(cuts.at[partner[1]], pieces.at[c], panel_send.at[i], panel_recv.at[i], partner))
     occ_copy.wait()
     for i in range(64):
         lines[i:i + 1, :] = occ_v[:, i * 128:(i + 1) * 128].astype(F32)
@@ -148,14 +160,14 @@
     own = pl.ds(pl.multiple_of((2 + core) * COLS, COLS), COLS)
     far_copies = []
     for h in (0, 1):
-        far[h, own, :] = dot(takes[h], panels[...]).astype(BF)
+        far[h, own, :] = pieces[:, h, :].astype(BF)
         for n, (partner, source_there) in enumerate(zip(far_partners, (2, 2, 0, 0, 1))):
             rows = pl.ds(pl.multiple_of((2 * source_there + core) * COLS, COLS), COLS)
             far_copies.append(send(far.at[h, own, :], far.at[h, rows, :], far_send.at[h, n], far_recv.at[h, n],
                                    partner))
 
     occ_copies = [send(occ_all.at[c], occ_all.at[c], occ_send.at[i], occ_recv.at[i], in_plane(i))
-                  for i in range(1, COLS)]
+                  for i in NEIGHBOURS]
 
     for copy in ask_copies:
         copy.wait()
@@ -194,7 +206,7 @@
         copy.wait()
     chosen[0, c] = dot(picks, near[0]).astype(BF)
     even_copies = [send(chosen.at[0, c], chosen.at[0, c], even_send.at[i], even_recv.at[i], in_plane(i))
-                   for i in range(1, COLS)]
+                   for i in NEIGHBOURS]
     for copy in near_copies[n_near:]:
         copy.wait()
     chosen[1, c] = dot(picks, near[1]).astype(BF)
@@ -202,7 +214,7 @@
     for p in range(PARTS):
         rows = pl.ds(p * PART, PART)
         odd_copies += [send(chosen.at[1, c, rows, :], chosen.at[1, c, rows, :], odd_send.at[p, i], odd_recv.at[p, i],
-                            in_plane(i)) for i in range(1, COLS)]
+                            in_plane(i)) for i in NEIGHBOURS]
 
     low = iota((32, 128), 1) < 64
 
@@ -248,19 +260,20 @@
             pltpu.VMEM((1, 4096), BF),
             pltpu.VMEM((64, 128), F32),
             pltpu.VMEM((T, 4096), BF),
-            pltpu.VMEM((32 * STEP, 128), F32),
+            pltpu.VMEM((33 * STEP, 128), F32),
             pltpu.VMEM((COLS, 64, 128), BF),
             pltpu.VMEM((COLS, 128, 64), BF),
             pltpu.VMEM((T, 64, 128), BF),
-            pltpu.VMEM((COLS * 32, 128), BF),
+            pltpu.VMEM((COLS, 2, 128), F32),
+            pltpu.VMEM((COLS, 2, 128), F32),
             pltpu.VMEM((2, 128, 128), BF),
             pltpu.VMEM((ENTRIES, 128), BF),
             pltpu.VMEM((ENTRIES, 128), BF),
             pltpu.VMEM((2, ENTRIES, 128), BF),
             pltpu.VMEM((2, PADDED, 128), BF),
             pltpu.VMEM((2, COLS, T, 128), BF),
-            pltpu.VMEM((2, COLS * STEP, 128), F32),
-            pltpu.VMEM((64 * STEP, 128), F32),
+            pltpu.VMEM((2, (COLS + 1) * STEP, 128), F32),
+            pltpu.VMEM((65 * STEP, 128), F32),
             dma((6,)), pltpu.SemaphoreType.REGULAR((4,)),
             dma((COLS,)), dma((COLS,)), dma((COLS,)), dma((COLS,)),
             dma((2, 5)), dma((2, 5)), dma((SERVED,)), dma((SERVED,)),

time: 57 us -> 54.3 us (0.953)
  the two profiles are of different devices: /device:TPU:8 before, /device:TPU:2 now
where the time goes in v3:
time: 54.3 us; the launch traced here: 54.1 us
  Pallas kernels  53.1 us (98%)
  local copies, waits for them, and re-layouts  0.97 us (2%)
    pallas_call x1, Pallas kernels, on_device(): pl.pallas_call(kernel, out_shape=pltpu.VMEM((T, 8192), BF), in_specs=[hbm...  53.1 us

profile of v3, /device:TPU:2, one launch (start us, length us, event | category | flops | bytes accessed | tf_op | source)
XLA Modules:
  0.0 54.1 jit_solution(11518667795584201390)
XLA Ops:
  0.0 53.1 %shard_map.55 = bf16[64,8192]{1,0:T(8,128)(2,1)S(1)} custom-call(bf16[64,4096]{1,0:T(8,128)(2,1)} %tensor.1, bf16[1,8192]{1,0:T(2,128)(2,1)} %occ.1, bf16[1,4096]{1,0:T(2,128)(2,1)} %virt.1, s32[1,64]{1,0:T(1,128)} %bitcast.3, s32[2,64]{1,0:T(2,128)} %bitcast.2), custom_call_target="tpu_custom_call" | custom-call | flops 300000000 | bytes 3000000 | tf_op jit(solution)/shard_map/pallas_call | solution.py:250
  53.1 1.0 %copy.7 = bf16[64,8192]{1,0:T(8,128)(2,1)} copy(bf16[64,8192]{1,0:T(8,128)(2,1)S(1)} %shard_map.55) | data formatting | bytes 2097152

commit v4 on v3

--- a/solution.py
+++ b/solution.py
@@ -108,10 +108,6 @@
     for i in NEIGHBOURS:
         partner = in_plane(i)
         panel_copies.append(send(cuts.at[partner[1]], pieces.at[c], panel_send.at[i], panel_recv.at[i], partner))
-    occ_copy.wait()
-    for i in range(64):
-        lines[i:i + 1, :] = occ_v[:, i * 128:(i + 1) * 128].astype(F32)
-    occ_all[c] = lines[...].astype(BF)
 
     owner_copy.wait()
     local_copy.wait()
@@ -148,10 +144,6 @@
         far[h, 96:128, :] = jnp.zeros((32, 128), BF)
         near[h, ENTRIES:, :] = jnp.zeros((PADDED - ENTRIES, 128), BF)
 
-    tensor_copy.wait()
-    for i in range(32):
-        tensor_f[i * STEP:i * STEP + T, :] = tensor_v[:, i * 128:(i + 1) * 128].astype(F32)
-
     for copy in panel_copies:
         copy.wait()
     for n in range(len(relays)):
@@ -166,8 +158,16 @@
             far_copies.append(send(far.at[h, own, :], far.at[h, rows, :], far_send.at[h, n], far_recv.at[h, n],
                                    partner))
 
+    occ_copy.wait()
+    for i in range(64):
+        lines[i:i + 1, :] = occ_v[:, i * 128:(i + 1) * 128].astype(F32)
+    occ_all[c] = lines[...].astype(BF)
     occ_copies = [send(occ_all.at[c], occ_all.at[c], occ_send.at[i], occ_recv.at[i], in_plane(i))
                   for i in NEIGHBOURS]
+
+    tensor_copy.wait()
+    for i in range(32):
+        tensor_f[i * STEP:i * STEP + T, :] = tensor_v[:, i * 128:(i + 1) * 128].astype(F32)
 
     for copy in ask_copies:
         copy.wait()

time: 54.3 us -> 54.3 us (level)
  no operation moved by 1% of the time
where the time goes in v4:
time: 54.3 us; the launch traced here: 54.1 us
  Pallas kernels  53.1 us (98%)
  local copies, waits for them, and re-layouts  0.97 us (2%)
    pallas_call x1, Pallas kernels, on_device(): pl.pallas_call(kernel, out_shape=pltpu.VMEM((T, 8192), BF), in_specs=[hbm...  53.1 us

profile of v4, /device:TPU:2, one launch (start us, length us, event | category | flops | bytes accessed | tf_op | source)
XLA Modules:
  0.0 54.1 jit_solution(2282525027910124338)
XLA Ops:
  0.0 53.1 %shard_map.55 = bf16[64,8192]{1,0:T(8,128)(2,1)S(1)} custom-call(bf16[64,4096]{1,0:T(8,128)(2,1)} %tensor.1, bf16[1,8192]{1,0:T(2,128)(2,1)} %occ.1, bf16[1,4096]{1,0:T(2,128)(2,1)} %virt.1, s32[1,64]{1,0:T(1,128)} %bitcast.3, s32[2,64]{1,0:T(2,128)} %bitcast.2), custom_call_target="tpu_custom_call" | custom-call | flops 300000000 | bytes 3000000 | tf_op jit(solution)/shard_map/pallas_call | solution.py:250
  53.2 1.0 %copy.7 = bf16[64,8192]{1,0:T(8,128)(2,1)} copy(bf16[64,8192]{1,0:T(8,128)(2,1)S(1)} %shard_map.55) | data formatting | bytes 2097152
